TPU v7x, 32 devices: a whole 2x2x4 slice. The times are simulated.
32 devices in a mesh: ctx: 8 (over y, x, core), exp: 4 (over z).
Axes of the slice: x: 2, y: 2, z: 4, core: 2. Of those that a mesh axis runs over, the one named last changes fastest.
Arguments:
- stream: bfloat16 [1024, 4096], P(('ctx', 'exp')), may hold values from -3 to 3
- queries: bfloat16 [1024, 4096], P('ctx', 'exp'), may hold values from -108 to 108
- attn_keys: bfloat16 [1024, 1024], P('ctx', 'exp'), may hold values from -3 to 3
- attn_values: bfloat16 [1024, 1024], P('ctx', 'exp'), may hold values from -6 to 6
- out_weight: bfloat16 [4096, 4096], P('exp'), may hold values from -0.09375 to 0.09375
- norm_gain: float32 [4096], replicated, may hold values from 0.25 to 1.75
- expert_ids: int32 [1024, 2], P(('ctx', 'exp')), may hold values from 0 to 3, all different within a row; in each aligned block of 32 rows (0 to 31, 32 to 63, ...) at most 32 rows name the same one
- combine: float32 [1024, 2], P(('ctx', 'exp')), may hold values from 0.1 to 0.9
- w_gate: bfloat16 [4, 4096, 14336], P('exp', None, 'ctx'), may hold values from -0.09375 to 0.09375
- w_up: bfloat16 [4, 4096, 14336], P('exp', None, 'ctx'), may hold values from -0.09375 to 0.09375
- w_down: bfloat16 [4, 14336, 4096], P('exp', 'ctx'), may hold values from -0.046875 to 0.046875
Outputs:
- layer_out: bfloat16 [1024, 4096], P(('ctx', 'exp'))
Inputs may be any that keep to these rules, and one draw needn't show every extreme that they name: `expert_ids`: taking the rows in aligned blocks of 32 (the rows of one device), no expert is named by more than 32 rows of a block, and in every draw some block names some expert exactly 32 times. The 2 experts of a row differ.
All inputs are finite; a program needn't handle non-finite values.
Results may differ from a plain program's by a relative error of at most 0.015.
Values may be sent and summed in bfloat16 or wider, within the bound.
No kernel may reach another device: no remote copies, remote signals or barrier semaphores. Data moves between devices by JAX's collectives and lax.ppermute only.
A program may use at most 128 MiB of HBM per device.

v0:
```python
import math

import jax
import jax.numpy as jnp
from jax import lax
from jax.sharding import PartitionSpec as P

HEAD_DIM = 128
TOP = 2
GROUP = 4


neg_big = -1e30


def absorb_block(carried, kv_block, queries_grid, query_pos):
    run_max, run_total, run_acc = carried
    key_rows = kv_block.shape[1]
    kv_heads_dev = queries_grid.shape[1]
    key_block = kv_block[0].reshape(key_rows, kv_heads_dev, HEAD_DIM)
    value_block = kv_block[1].reshape(key_rows, kv_heads_dev, HEAD_DIM)
    scores = jnp.einsum(
        "tkgd,ukd->kgtu", queries_grid, key_block, preferred_element_type=jnp.float32
    ) * (1.0 / math.sqrt(HEAD_DIM))
    key_pos = jnp.arange(key_rows, dtype=jnp.int32)
    allowed = query_pos[:, None] >= key_pos[None, :]
    scores = jnp.where(allowed, scores, neg_big)
    new_max = jnp.maximum(run_max, jnp.max(scores, axis=-1))
    weights = jnp.where(allowed, jnp.exp(scores - new_max[..., None]), 0.0)
    new_total = jnp.sum(weights, axis=-1)
    contrib = jnp.einsum(
        "kgtu,ukd->tkgd",
        weights.astype(jnp.bfloat16),
        value_block,
        preferred_element_type=jnp.float32,
    )
    return (new_max, new_total, contrib)


def rms_norm(values_f32, norm_gain):
    mean_square = jnp.mean(values_f32 * values_f32, axis=-1, keepdims=True)
    return (values_f32 * lax.rsqrt(mean_square + 1e-05) * norm_gain).astype(jnp.bfloat16)


def slot_table(expert_ids, n_exp, capacity):
    flat_ids = expert_ids.reshape(-1)
    onehot = (flat_ids[:, None] == jnp.arange(n_exp, dtype=jnp.int32)[None, :]).astype(jnp.int32)
    before = jnp.cumsum(onehot, axis=0) - onehot
    slot_rank = jnp.sum(before * onehot, axis=1)
    return flat_ids * capacity + slot_rank


def pick_rows(slot_index, token_count, n_slots, normed):
    chosen = slot_index[None, :] == jnp.arange(n_slots, dtype=jnp.int32)[:, None]
    chosen = jnp.sum(chosen.reshape(n_slots, token_count, TOP).astype(jnp.float32), axis=2)
    return jnp.dot(chosen.astype(jnp.bfloat16), normed, preferred_element_type=jnp.float32).astype(
        jnp.bfloat16
    )


def body(
    stream,
    queries,
    attn_keys,
    attn_values,
    out_weight,
    norm_gain,
    expert_ids,
    combine,
    w_gate,
    w_up,
    w_down,
):
    span = queries.shape[0]
    n_exp = lax.axis_size("exp")
    ctx_pos = lax.axis_index("ctx")
    tok_rows = stream.shape[0]
    model_dim = stream.shape[1]
    capacity = max(2, 4 * span // (n_exp * n_exp))
    n_slots = n_exp * capacity
    kv_heads_dev = attn_keys.shape[1] // HEAD_DIM
    queries_grid = queries.reshape(span, kv_heads_dev, GROUP, HEAD_DIM)
    query_pos = ctx_pos * span + jnp.arange(span, dtype=jnp.int32)
    kv_pair = jnp.stack([attn_keys, attn_values])
    start_carry = (
        jnp.full((kv_heads_dev, GROUP, span), neg_big, jnp.float32),
        jnp.zeros((kv_heads_dev, GROUP, span), jnp.float32),
        jnp.zeros((span, kv_heads_dev, GROUP, HEAD_DIM), jnp.float32),
    )
    last_query = ctx_pos * span + span - 1
    kv_piece = lax.all_gather(kv_pair, "ctx", axis=1, tiled=True)
    carried = lax.cond(
        jnp.int32(0) <= last_query,
        lambda inner_state: absorb_block(inner_state, kv_piece, queries_grid, query_pos),
        lambda inner_state: inner_state,
        start_carry,
    )
    run_max, run_total, run_acc = carried
    attention = (
        (run_acc / jnp.transpose(run_total, (2, 0, 1))[..., None])
        .reshape(span, kv_heads_dev * GROUP * HEAD_DIM)
        .astype(jnp.bfloat16)
    )
    slot_index = slot_table(expert_ids, n_exp, capacity)
    mixed = stream.astype(jnp.float32) + lax.psum_scatter(
        jnp.dot(attention, out_weight, preferred_element_type=jnp.float32).astype(jnp.bfloat16),
        "exp",
        scatter_dimension=0,
        tiled=True,
    ).astype(jnp.float32)
    normed = rms_norm(mixed, norm_gain)
    outgoing = pick_rows(slot_index, tok_rows, n_slots, normed)
    rows_in = lax.all_to_all(
        outgoing.reshape(n_exp, capacity, model_dim), "exp", split_axis=0, concat_axis=0, tiled=True
    ).reshape(n_slots, model_dim)
    gate_mat = w_gate[0]
    up_mat = w_up[0]
    down_mat = w_down[0]
    row_piece = lax.all_gather(rows_in, "ctx", axis=0, tiled=True)
    gate_part = jnp.dot(row_piece, gate_mat, preferred_element_type=jnp.float32)
    up_part = jnp.dot(row_piece, up_mat, preferred_element_type=jnp.float32)
    hidden_all = (jax.nn.silu(gate_part) * up_part).astype(jnp.bfloat16)
    expert_result = lax.psum_scatter(
        jnp.dot(hidden_all, down_mat, preferred_element_type=jnp.float32).astype(jnp.bfloat16),
        "ctx",
        scatter_dimension=0,
        tiled=True,
    )
    returned = lax.all_to_all(
        expert_result.reshape(n_exp, capacity, model_dim),
        "exp",
        split_axis=0,
        concat_axis=0,
        tiled=True,
    ).reshape(n_slots, model_dim)
    picked = (
        jnp.take(returned, slot_index, axis=0).reshape(tok_rows, TOP, model_dim).astype(jnp.float32)
    )
    layer_out = (mixed + jnp.sum(combine[..., None] * picked, axis=1)).astype(jnp.bfloat16)
    return layer_out


def solution(mesh):
    in_specs = (
        P(("ctx", "exp"), None),
        P("ctx", "exp"),
        P("ctx", "exp"),
        P("ctx", "exp"),
        P("exp", None),
        P(),
        P(("ctx", "exp"), None),
        P(("ctx", "exp"), None),
        P("exp", None, "ctx"),
        P("exp", None, "ctx"),
        P("exp", "ctx", None),
    )
    out_specs = P(("ctx", "exp"), None)
    return jax.shard_map(body, mesh=mesh, in_specs=in_specs, out_specs=out_specs, check_vma=False)
```

profile of v0, /device:TPU:0, one launch (start us, length us, event | category | flops | bytes accessed | tf_op | source)
XLA Modules:
  0.0 341.0 jit_solution(5388504992323487978)
XLA Ops:
  6.5 0.9 copy.43
  7.5 1.0 copy.44
  8.5 0.7 pad_maximum_fusion
  9.2 26.4 %all-gather.3.cloned.1.call-done = bf16[2,1024,256]{1,2,0:T(8,128)(2,1)} async-done(((bf16[2,128,256]{1,2,0:T(8,128)(2,1)}), bf16[2,1024,256]{1,2,0:T(8,128)(2,1)}) %all-gather.3.cloned.1.call-update) | async-done | bytes 1048592 | tf_op jit(solution)/shard_map/all_gather | solution.py:91
  35.6 10.2 %conditional.1 = (f32[2,4,128]{2,1,0:T(4,128)S(1)}, f32[128,2,4,128]{0,3,2,1:T(8,128)S(1)}) conditional(s32[]{:T(128)} %convert_element_type.49, () %tuple.13, (s32[]{:T(128)}, s32[128]{0:T(128)S(1)}, bf16[2,1024,256]{1,2,0:T(8,128)(2,1)}, bf16[128,1024]{1,0:T(8,128)(2,1)}) %tuple.14), branch_computations={%region_0.0_spmd, %region_1.4_spmd} | conditional | flops 550632576 | bytes 35415600 | solution.py:92
  35.7 1.3 fusion.32
  37.0 1.1 reshape.90
  38.1 0.9 fusion
  39.0 1.9 copy-done
  40.9 1.5 fusion.6
  42.4 0.2 copy.59
  42.6 3.2 fusion.2
  45.9 5.7 %convolution_convert_fusion.1 = bf16[128,4096]{1,0:T(8,128)(2,1)} fusion(bf16[128,1024]{0,1:T(8,128)(2,1)S(1)} %bitcast.64, bf16[1024,4096]{1,0:T(8,128)(2,1)} %param.17), kind=kOutput, calls=%fused_computation.26 | convolution fusion | flops 1074266112 | bytes 9699328 | tf_op jit(solution)/shard_map/dot_general | solution.py:106
  52.1 0.2 select_reduce_fusion
  52.3 0.1 reduce_sum.50
  52.5 26.4 %reduce-scatter.3.cloned.1.call-done = bf16[32,4096]{1,0:T(8,128)(2,1)} async-done(((bf16[128,4096]{1,0:T(8,128)(2,1)}), bf16[32,4096]{1,0:T(8,128)(2,1)}) %reduce-scatter.3.cloned.1.call-update) | async-done | bytes 262160 | tf_op jit(solution)/shard_map/reduce_scatter | solution.py:105
  79.0 1.1 multiply_reduce_fusion.1
  80.1 1.4 convolution_convert_fusion
  81.6 29.0 %all_to_all.10 = bf16[4,32,4096]{2,1,0:T(8,128)(2,1)} all-to-all(bf16[4,32,4096]{2,1,0:T(8,128)(2,1)S(1)} %bitcast.62), channel_id=1, replica_groups=mesh['ctx'=8,'exp'=4] {'exp'}, dimensions={0} | all-to-all | bytes 2097152 | tf_op jit(solution)/shard_map/all_to_all | solution.py:113
  110.6 0.2 reduce-scatter.5.cloned.1.call-start
  110.8 53.4 %all-gather.5.cloned.1.call-done = bf16[1024,4096]{1,0:T(8,128)(2,1)} async-done(((bf16[128,4096]{1,0:T(8,128)(2,1)}), bf16[1024,4096]{1,0:T(8,128)(2,1)}) %all-gather.5.cloned.1.call-update) | async-done | bytes 8388624 | tf_op jit(solution)/shard_map/all_gather | solution.py:119
  164.2 21.8 %fusion.18 = f32[1024,1792]{1,0:T(8,128)} fusion(bf16[1024,4096]{1,0:T(8,128)(2,1)} %all-gather.5.cloned.1.call-done, bf16[1,4096,1792]{2,1,0:T(8,128)(2,1)} %param.21), kind=kOutput, calls=%fused_computation.21 | convolution fusion | flops 15032385536 | bytes 30408704 | tf_op jit(solution)/shard_map/dot_general | solution.py:120
  186.0 23.5 %multiply_convert_fusion = bf16[1024,1792]{1,0:T(8,128)(2,1)} fusion(f32[1024,1792]{1,0:T(8,128)} %fusion.18, bf16[1024,4096]{1,0:T(8,128)(2,1)} %all-gather.5.cloned.1.call-done, bf16[1,4096,1792]{2,1,0:T(8,128)(2,1)} %param.22), kind=kOutput, calls=%fused_computation.24 | convolution fusion | flops 15043395584 | bytes 34078720 | tf_op jit(solution)/shard_map/dot_general | solution.py:121
  209.5 19.4 %fusion.20 = bf16[1024,4096]{1,0:T(8,128)(2,1)} fusion(bf16[1024,1792]{1,0:T(8,128)(2,1)} %multiply_convert_fusion, bf16[1,1792,4096]{2,1,0:T(8,128)(2,1)S(1)} %bitcast.71), kind=kOutput, calls=%fused_computation.23 | convolution fusion | flops 15036579840 | bytes 26738688 | tf_op jit(solution)/shard_map/dot_general | solution.py:124
  228.9 71.4 %reduce-scatter.5.cloned.1.call-done = bf16[128,4096]{1,0:T(8,128)(2,1)} async-done(((bf16[1024,4096]{1,0:T(8,128)(2,1)}), bf16[128,4096]{1,0:T(8,128)(2,1)}) %reduce-scatter.5.cloned.1.call-update) | async-done | bytes 1048592 | tf_op jit(solution)/shard_map/reduce_scatter | solution.py:123
  300.4 4.6 %all-to-all-start.1 = ((bf16[4,32,4096]{2,1,0:T(8,128)(2,1)}), bf16[4,32,4096]{2,1,0:T(8,128)(2,1)S(1)}, u32[]{:S(2)}, u32[]{:S(2)}) async-start(bf16[4,32,4096]{2,1,0:T(8,128)(2,1)} %bitcast.65), calls=%async_computation.3 | async-start | bytes 2097152 | tf_op jit(solution)/shard_map/all_to_all | solution.py:129
  305.1 0.1 copy.49
  305.4 25.3 %all-to-all-done.1 = bf16[4,32,4096]{2,1,0:T(8,128)(2,1)S(1)} async-done(((bf16[4,32,4096]{2,1,0:T(8,128)(2,1)}), bf16[4,32,4096]{2,1,0:T(8,128)(2,1)S(1)}, u32[]{:S(2)}, u32[]{:S(2)}) %all-to-all-start.1) | async-done | bytes 1048608 | tf_op jit(solution)/shard_map/all_to_all | solution.py:129
  330.7 0.9 gather_fusion
  331.6 0.3 gather.7
  331.9 1.8 multiply_reduce_fusion
  333.7 0.8 add_convert_fusion
  (46 shorter events, 1.2 us)
Async XLA Ops:
  6.5 29.0 %all-gather.3.cloned.1.call-start = ((), (), s32[]{:S(2)}) async-start(), calls=%async_computation.4 | async-start | bytes 1179648 | tf_op jit(solution)/shard_map/all_gather | solution.py:91
  9.2 69.8 %reduce-scatter.3.cloned.1.call-start = ((), (), s32[]{:S(2)}) async-start(), calls=%async_computation.5 | async-start | bytes 1310720 | tf_op jit(solution)/shard_map/reduce_scatter | solution.py:105
  38.9 1.9 copy-start
  45.9 5.8 %copy-start.4 = (s32[32,2]{0,1:T(2,128)S(1)}, s32[32,2]{0,1:T(2,128)}, u32[]{:S(2)}) copy-start(s32[32,2]{0,1:T(2,128)} %param.19) | copy-start | bytes 772
  45.9 33.1 %copy-start.1 = (bf16[32,4096]{1,0:T(8,128)(2,1)S(1)}, bf16[32,4096]{1,0:T(8,128)(2,1)}, u32[]{:S(2)}) copy-start(bf16[32,4096]{1,0:T(8,128)(2,1)} %param.13) | copy-start | bytes 786436
  45.9 34.2 %copy-start.3 = (f32[4096]{0:T(1024)S(1)}, f32[4096]{0:T(1024)}, u32[]{:S(2)}) copy-start(f32[4096]{0:T(1024)} %param.18) | copy-start | bytes 49156
  51.6 112.6 %all-gather.5.cloned.1.call-start = ((), (), s32[]{:S(2)}) async-start(), calls=%async_computation.6 | async-start | bytes 9437184 | tf_op jit(solution)/shard_map/all_gather | solution.py:119
  110.6 189.8 %reduce-scatter.5.cloned.1.call-start = ((), (), s32[]{:S(2)}) async-start(), calls=%async_computation.7 | async-start | bytes 9437184 | tf_op jit(solution)/shard_map/reduce_scatter | solution.py:123
  164.2 45.3 %slice-start = ((s8[14680064]{0:T(1024)(128)(4,1)}), s8[4194304]{0:T(1024)(128)(4,1)S(1)}, s32[]{:S(2)}) async-start(s8[14680064]{0:T(1024)(128)(4,1)} %bitcast.70), calls=%async_computation.8 | async-start | bytes 8388608
  164.2 45.3 %slice-start.1 = ((s8[14680064]{0:T(1024)(128)(4,1)}), s8[4194304]{0:T(1024)(128)(4,1)S(1)}, s32[]{:S(2)}) async-start(s8[14680064]{0:T(1024)(128)(4,1)} %bitcast.70), calls=%async_computation.9 | async-start | bytes 8388608
  186.0 23.5 %slice-start.2 = ((s8[14680064]{0:T(1024)(128)(4,1)}), s8[4194304]{0:T(1024)(128)(4,1)S(1)}, s32[]{:S(2)}) async-start(s8[14680064]{0:T(1024)(128)(4,1)} %bitcast.70), calls=%async_computation.10 | async-start | bytes 8388608
  186.0 23.5 %slice-start.3 = ((s8[14680064]{0:T(1024)(128)(4,1)}), s8[2097152]{0:T(1024)(128)(4,1)S(1)}, s32[]{:S(2)}) async-start(s8[14680064]{0:T(1024)(128)(4,1)} %bitcast.70), calls=%async_computation.11 | async-start | bytes 4194304
  228.9 76.4 %copy-start.5 = (f32[32,2]{0,1:T(2,128)S(1)}, f32[32,2]{0,1:T(2,128)}, u32[]{:S(2)}) copy-start(f32[32,2]{0,1:T(2,128)} %param.20) | copy-start | bytes 772
  228.9 104.8 %copy-start.2 = (bf16[32,4096]{1,0:T(8,128)(2,1)S(1)}, bf16[32,4096]{1,0:T(8,128)(2,1)}, u32[]{:S(2)}) copy-start(bf16[32,4096]{1,0:T(8,128)(2,1)} %reduce-scatter.3.cloned.1.call-done) | copy-start | bytes 786436
  300.4 30.3 %all-to-all-start.1 = ((bf16[4,32,4096]{2,1,0:T(8,128)(2,1)}), bf16[4,32,4096]{2,1,0:T(8,128)(2,1)S(1)}, u32[]{:S(2)}, u32[]{:S(2)}) async-start(bf16[4,32,4096]{2,1,0:T(8,128)(2,1)} %bitcast.65), calls=%async_computation.3 | async-start | bytes 2097152 | tf_op jit(solution)/shard_map/all_to_all | solution.py:129
Sparse Core Ops, SparseCore 0:
  9.3 26.2 all-gather.2
  51.8 27.1 reduce-scatter.2
  110.7 53.4 all-gather.4
  229.0 71.2 reduce-scatter.4
where the time goes:
time: 341 us
  waiting for transfers between devices  203 us (60%)
  matrix products  74.2 us (22%)
  blocking collectives  29 us (9%)
  between operations  13.3 us (4%)
  local copies, waits for them, and re-layouts  8.43 us (2%)
  other arithmetic  8.19 us (2%)
  starting transfers between devices  4.89 us (1%)
    reduce_scatter x1, waiting for transfers between devices, body(): lax.psum_scatter(jnp.dot(hidden_all, down_mat, preferred_element_type=jnp...  71.4 us
    all_gather x1, waiting for transfers between devices, body(): row_piece = lax.all_gather(rows_in, 'ctx', axis=0, tiled=True)  53.4 us
    all_to_all x1, blocking collectives, body(): lax.all_to_all(outgoing.reshape(n_exp, capacity, model_dim), 'exp', split...  29 us
    reduce_scatter x1, waiting for transfers between devices, body(): lax.psum_scatter(jnp.dot(attention, out_weight, preferred_element_type=jn...  26.4 us
    all_gather x1, waiting for transfers between devices, body(): kv_piece = lax.all_gather(kv_pair, 'ctx', axis=1, tiled=True)  26.4 us
    all_to_all x1, waiting for transfers between devices, body(): lax.all_to_all(expert_result.reshape(n_exp, capacity, model_dim), 'exp',...  25.3 us
    dot_general x1, matrix products, body(): up_part = jnp.dot(row_piece, up_mat, preferred_element_type=jnp.float32)  23.5 us
    dot_general x1, matrix products, body(): gate_part = jnp.dot(row_piece, gate_mat, preferred_element_type=jnp.float32)  21.8 us
  transfers between devices with their start and end apart: 5, of which 5 were waited for; matrix products, arithmetic and copies ran while one was open for 0% of the time, Pallas kernels for 0%

commit v1 on v0

v1 whole, which is shorter than its diff:
```python
import functools
import math

import jax
import jax.numpy as jnp
from jax import lax
from jax.experimental import pallas as pl
from jax.experimental.pallas import tpu as pltpu
from jax.sharding import PartitionSpec as P

HEAD_DIM = 128
TOP = 2
GROUP = 4
MASKED = -1e30
MIB = 1 << 20


def swap(value, axis, mask):
    count = lax.axis_size(axis)
    return lax.ppermute(value, axis, [(i, i ^ mask) for i in range(count)])


def attend_kernel(
    n_exp, tok_rows, where_ref, q_ref, near_ref, far_ref, weight_hbm, *rest
):
    outs, (att_ref, sorted_ref, weight_ref, weight_sem) = rest[:n_exp], rest[n_exp:]
    fetch = pltpu.make_async_copy(weight_hbm, weight_ref, weight_sem)
    fetch.start()
    span = q_ref.shape[0]
    kv_width = near_ref.shape[1] // 2
    kv_heads = kv_width // HEAD_DIM
    ctx_pos, exp_pos = where_ref[0], where_ref[1]
    n_keys = near_ref.shape[0]
    query_pos = ctx_pos * span + lax.broadcasted_iota(jnp.int32, (span, n_keys), 0)
    column = lax.broadcasted_iota(jnp.int32, (span, n_keys), 1)
    block, within = column // span, column % span
    masks = []
    for core in range(2):
        key_pos = (ctx_pos ^ (2 * block + core)) * span + within
        masks.append(query_pos >= key_pos)
    scale = 1.0 / math.sqrt(HEAD_DIM)
    for g in range(kv_heads):
        keys = slice(g * HEAD_DIM, (g + 1) * HEAD_DIM)
        values = slice(kv_width + g * HEAD_DIM, kv_width + (g + 1) * HEAD_DIM)
        for r in range(GROUP):
            h = g * GROUP + r
            q = q_ref[:, h * HEAD_DIM : (h + 1) * HEAD_DIM]
            scores = []
            for ref, mask in zip((near_ref, far_ref), masks):
                s = lax.dot_general(
                    q, ref[:, keys], (((1,), (1,)), ((), ())), preferred_element_type=jnp.float32
                )
                scores.append(jnp.where(mask, s * scale, MASKED))
            top = jnp.maximum(
                jnp.max(scores[0], axis=1, keepdims=True), jnp.max(scores[1], axis=1, keepdims=True)
            )
            total = jnp.zeros((span, 1), jnp.float32)
            acc = jnp.zeros((span, HEAD_DIM), jnp.float32)
            for ref, s in zip((near_ref, far_ref), scores):
                w = jnp.exp(s - top)
                total = total + jnp.sum(w, axis=1, keepdims=True)
                acc = acc + jnp.dot(
                    w.astype(jnp.bfloat16), ref[:, values], preferred_element_type=jnp.float32
                )
            att_ref[:, h * HEAD_DIM : (h + 1) * HEAD_DIM] = (acc / total).astype(jnp.bfloat16)
    for k in range(n_exp):
        first = pl.multiple_of((exp_pos ^ k) * tok_rows, tok_rows)
        sorted_ref[k * tok_rows : (k + 1) * tok_rows, :] = att_ref[pl.ds(first, tok_rows), :]
    fetch.wait()
    model_dim = weight_ref.shape[1]
    tile = min(1024, model_dim)
    for lo in range(0, model_dim, tile):
        part = jnp.dot(
            sorted_ref[...], weight_ref[:, lo : lo + tile], preferred_element_type=jnp.float32
        ).astype(jnp.bfloat16)
        for k in range(n_exp):
            outs[k][:, lo : lo + tile] = part[k * tok_rows : (k + 1) * tok_rows]


def attend(where, queries, near, far, out_weight, n_exp, tok_rows):
    span = queries.shape[0]
    model_dim = out_weight.shape[1]
    vmem = pl.BlockSpec(memory_space=pltpu.VMEM)
    return pl.pallas_call(
        functools.partial(attend_kernel, n_exp, tok_rows),
        out_shape=[jax.ShapeDtypeStruct((tok_rows, model_dim), jnp.bfloat16)] * n_exp,
        in_specs=[
            pl.BlockSpec(memory_space=pltpu.SMEM),
            vmem,
            vmem,
            vmem,
            pl.BlockSpec(memory_space=pl.ANY),
        ],
        out_specs=[vmem] * n_exp,
        scratch_shapes=[
            pltpu.VMEM(queries.shape, jnp.bfloat16),
            pltpu.VMEM(queries.shape, jnp.bfloat16),
            pltpu.VMEM(out_weight.shape, jnp.bfloat16),
            pltpu.SemaphoreType.DMA(()),
        ],
        compiler_params=pltpu.CompilerParams(vmem_limit_bytes=40 * MIB),
        cost_estimate=pl.CostEstimate(
            flops=8 * 1000 * 1000 * 1000, bytes_accessed=12 * MIB, transcendentals=MIB
        ),
        name="attend",
    )(where, queries, near, far, out_weight)


def norm_kernel(stream_ref, gain_ref, *rest):
    parts, (mixed_ref, normed_ref) = rest[:-2], rest[-2:]
    mixed = stream_ref[...].astype(jnp.float32)
    update = parts[0][...].astype(jnp.float32)
    for part in parts[1:]:
        update = update + part[...].astype(jnp.float32)
    mixed = mixed + update
    mixed_ref[...] = mixed
    mean_square = jnp.mean(mixed * mixed, axis=-1, keepdims=True)
    normed_ref[...] = (mixed * lax.rsqrt(mean_square + 1e-05) * gain_ref[...]).astype(jnp.bfloat16)


def add_and_norm(stream, norm_gain, parts):
    vmem = pl.BlockSpec(memory_space=pltpu.VMEM)
    return pl.pallas_call(
        norm_kernel,
        out_shape=[
            jax.ShapeDtypeStruct(stream.shape, jnp.float32),
            jax.ShapeDtypeStruct(stream.shape, jnp.bfloat16),
        ],
        in_specs=[vmem] * (2 + len(parts)),
        out_specs=[vmem] * 2,
        cost_estimate=pl.CostEstimate(
            flops=6 * stream.size, bytes_accessed=20 * stream.size, transcendentals=0
        ),
        name="add_and_norm",
    )(stream, norm_gain.reshape(1, -1), *parts)


def expert_kernel(n_parts, n_up, *refs):
    parts = refs[:n_parts]
    gate_ref, up_ref, down_ref, keep_ref, send_ref, rows_ref, hidden_ref, sems = refs[n_parts:]
    step = pl.program_id(0)
    rows = parts[0].shape[0]
    tile = gate_ref.shape[2]

    @pl.when(step == 0)
    def _():
        fetches = [
            pltpu.make_async_copy(part, rows_ref.at[pl.ds(i * rows, rows)], sems.at[i])
            for i, part in enumerate(parts)
        ]
        for fetch in fetches:
            fetch.start()
        for fetch in fetches:
            fetch.wait()

    @pl.when(step < n_up)
    def _():
        gate = jnp.dot(rows_ref[...], gate_ref[0], preferred_element_type=jnp.float32)
        up = jnp.dot(rows_ref[...], up_ref[0], preferred_element_type=jnp.float32)
        hidden = gate / (1.0 + jnp.exp(-gate)) * up
        first = pl.multiple_of(step * tile, tile)
        hidden_ref[:, pl.ds(first, tile)] = hidden.astype(jnp.bfloat16)

    @pl.when(step >= n_up)
    def _():
        result = jnp.dot(
            hidden_ref[...], down_ref[0], preferred_element_type=jnp.float32
        ).astype(jnp.bfloat16)
        half = keep_ref.shape[0]
        keep_ref[...] = result[:half]
        send_ref[...] = result[half:]


def expert_rows(parts, w_gate, w_up, w_down):
    n_parts, rows = len(parts), parts[0].shape[0]
    total = n_parts * rows
    _, model_dim, hidden_dim = w_gate.shape
    tile = 256 if hidden_dim % 256 == 0 else 128
    down_tile = 512
    n_up, n_down = hidden_dim // tile, model_dim // down_tile
    half = jax.ShapeDtypeStruct((total // 2, model_dim), jnp.bfloat16)
    up_spec = pl.BlockSpec((1, model_dim, tile), lambda j: (0, 0, jnp.minimum(j, n_up - 1)))
    out_spec = pl.BlockSpec((total // 2, down_tile), lambda j: (0, jnp.maximum(j - n_up, 0)))
    return pl.pallas_call(
        functools.partial(expert_kernel, n_parts, n_up),
        grid=(n_up + n_down,),
        out_shape=[half, half],
        in_specs=[pl.BlockSpec(memory_space=pl.ANY)] * n_parts
        + [
            up_spec,
            up_spec,
            pl.BlockSpec((1, hidden_dim, down_tile), lambda j: (0, 0, jnp.maximum(j - n_up, 0))),
        ],
        out_specs=[out_spec, out_spec],
        scratch_shapes=[
            pltpu.VMEM((total, model_dim), jnp.bfloat16),
            pltpu.VMEM((total, hidden_dim), jnp.bfloat16),
            pltpu.SemaphoreType.DMA((n_parts,)),
        ],
        compiler_params=pltpu.CompilerParams(vmem_limit_bytes=40 * MIB),
        cost_estimate=pl.CostEstimate(
            flops=6 * total * model_dim * hidden_dim,
            bytes_accessed=6 * model_dim * hidden_dim,
            transcendentals=total * hidden_dim,
        ),
        name="expert_rows",
    )(*parts, w_gate, w_up, w_down)


def add_bf16(*terms):
    total = terms[0].astype(jnp.float32)
    for term in terms[1:]:
        total = total + term.astype(jnp.float32)
    return total.astype(jnp.bfloat16)


def body(
    stream,
    queries,
    attn_keys,
    attn_values,
    out_weight,
    norm_gain,
    expert_ids,
    combine,
    w_gate,
    w_up,
    w_down,
):
    n_ctx, n_exp = lax.axis_size("ctx"), lax.axis_size("exp")
    ctx_pos, exp_pos = lax.axis_index("ctx"), lax.axis_index("exp")
    tok_rows = stream.shape[0]
    chips = range(2, n_ctx, 2)

    kv = jnp.concatenate([attn_keys, attn_values], axis=1)
    near = jnp.concatenate([kv] + [swap(kv, "ctx", m) for m in chips], axis=0)
    far = swap(near, "ctx", 1)
    where = jnp.stack([ctx_pos, exp_pos]).astype(jnp.int32)
    partial = attend(where, queries, near, far, out_weight, n_exp, tok_rows)
    arrived = [partial[0]] + [swap(partial[k], "exp", k) for k in range(1, n_exp)]
    mixed, normed = add_and_norm(stream, norm_gain, arrived)

    planes = [normed] + [swap(normed, "exp", k) for k in range(1, n_exp)]
    groups = [[k] for k in range(min(2, n_exp))]
    if n_exp > 2:
        groups.append(list(range(2, n_exp)))
    returned = {}
    for group in groups:
        own = planes[group[0]] if len(group) == 1 else jnp.concatenate([planes[k] for k in group])
        lane = [own] + [swap(own, "ctx", m) for m in chips]
        other = [swap(piece, "ctx", 1) for piece in lane]
        keep, send = expert_rows(lane + other, w_gate, w_up, w_down)
        got = swap(send, "ctx", 1)
        rows = own.shape[0]
        pieces = [
            add_bf16(keep[i * rows : (i + 1) * rows], got[i * rows : (i + 1) * rows])
            for i in range(len(lane))
        ]
        total = add_bf16(pieces[0], *[swap(p, "ctx", m) for p, m in zip(pieces[1:], chips)])
        for i, k in enumerate(group):
            piece = total[i * tok_rows : (i + 1) * tok_rows]
            returned[k] = swap(piece, "exp", k) if k else piece
    update = jnp.zeros(mixed.shape, jnp.float32)
    for k in range(n_exp):
        share = jnp.sum(jnp.where(expert_ids == (exp_pos ^ k), combine, 0.0), axis=1, keepdims=True)
        update = update + share * returned[k].astype(jnp.float32)
    return (mixed + update).astype(jnp.bfloat16)


def solution(mesh):
    in_specs = (
        P(("ctx", "exp"), None),
        P("ctx", "exp"),
        P("ctx", "exp"),
        P("ctx", "exp"),
        P("exp", None),
        P(),
        P(("ctx", "exp"), None),
        P(("ctx", "exp"), None),
        P("exp", None, "ctx"),
        P("exp", None, "ctx"),
        P("exp", "ctx", None),
    )
    out_specs = P(("ctx", "exp"), None)
    return jax.shard_map(body, mesh=mesh, in_specs=in_specs, out_specs=out_specs, check_vma=False)
```

time: 341 us -> 281 us (0.82)
  Pallas kernels: 0 us -> 86.8 us
  matrix products: 74.2 us -> 0 us
  waiting for transfers between devices: 203 us -> 132 us
  starting transfers between devices: 4.89 us -> 46.4 us
  blocking collectives: 29 us -> 0 us
  between operations: 13.3 us -> 0.22 us
    ppermute x0 -> x46, waiting for transfers between devices: none -> 132 us  [swap(): return lax.ppermute(value, axis, [(i, i ^ mask) for i in range(count)])]
    reduce_scatter x2 -> x0, waiting for transfers between devices: 97.9 us -> none  [the longest x1 71.4 us: body(): lax.psum_scatter(jnp.dot(hidden_all, down_mat, preferred_element_type=jnp...]
    pallas_call x0 -> x5, Pallas kernels: none -> 86.8 us  [the longest x3 79 us: expert_rows(): pl.pallas_call(functools.partial(expert_kernel, n_parts, n_up), grid=(n_u...]
    all_gather x2 -> x0, waiting for transfers between devices: 79.7 us -> none  [the longest x1 53.4 us: body(): row_piece = lax.all_gather(rows_in, 'ctx', axis=0, tiled=True)]
    dot_general x7 -> x0, matrix products: 74.2 us -> none  [the longest x1 23.5 us: body(): up_part = jnp.dot(row_piece, up_mat, preferred_element_type=jnp.float32)]
    ppermute x0 -> x46, starting transfers between devices: none -> 46.4 us  [swap(): return lax.ppermute(value, axis, [(i, i ^ mask) for i in range(count)])]
    all_to_all x1 -> x0, blocking collectives: 29 us -> none  [body(): lax.all_to_all(outgoing.reshape(n_exp, capacity, model_dim), 'exp', split...]
    all_to_all x1 -> x0, waiting for transfers between devices: 25.3 us -> none  [body(): lax.all_to_all(expert_result.reshape(n_exp, capacity, model_dim), 'exp',...]
  transfers between devices with their start and end apart: 5 -> 46, of which waited for: 5 -> 19; matrix products, arithmetic and copies ran while one was open for 0% -> 1% of each run, Pallas kernels for 0% -> 28%
where the time goes in v1:
time: 281 us; the launch traced here: 280 us
  waiting for transfers between devices  132 us (47%)
  Pallas kernels  86.8 us (31%)
  starting transfers between devices  46.4 us (17%)
  local copies, waits for them, and re-layouts  9.35 us (3%)
  other arithmetic  5.18 us (2%)
    ppermute x46, waiting for transfers between devices, swap(): return lax.ppermute(value, axis, [(i, i ^ mask) for i in range(count)])  132 us
    pallas_call x3, Pallas kernels, expert_rows(): pl.pallas_call(functools.partial(expert_kernel, n_parts, n_up), grid=(n_u...  79 us
    ppermute x46, starting transfers between devices, swap(): return lax.ppermute(value, axis, [(i, i ^ mask) for i in range(count)])  46.4 us
    unnamed x22, local copies, waits for them, and re-layouts  7.65 us
  transfers between devices with their start and end apart: 46, of which 19 were waited for; matrix products, arithmetic and copies ran while one was open for 1% of the time, Pallas kernels for 28%

profile of v1, /device:TPU:0, one launch (start us, length us, event | category | flops | bytes accessed | tf_op | source)
XLA Modules:
  0.0 280.3 jit_solution(16599161644720586349)
XLA Ops:
  1.7 3.9 %collective-permute-start.2 = (bf16[128,512]{1,0:T(8,128)(2,1)S(1)}, bf16[128,512]{1,0:T(8,128)(2,1)S(1)}, u32[]{:S(2)}, u32[]{:S(2)}) collective-permute-start(bf16[128,512]{1,0:T(8,128)(2,1)S(1)} %constant_dynamic-update-slice_fusion), channel_id=1, source_target_pairs={{0,24},{4,28},{8,16},{12,20},{16,8},{20,12},{24,0},{28,4},{1,25},{... | collective-permute-start | bytes 393224 | tf_op jit(solution)/shard_map/ppermute | solution.py:20
  6.2 3.3 %collective-permute-done.2 = bf16[128,512]{1,0:T(8,128)(2,1)S(1)} collective-permute-done((bf16[128,512]{1,0:T(8,128)(2,1)S(1)}, bf16[128,512]{1,0:T(8,128)(2,1)S(1)}, u32[]{:S(2)}, u32[]{:S(2)}) %collective-permute-start.2) | collective-permute-done | bytes 131104 | tf_op jit(solution)/shard_map/ppermute | solution.py:20
  9.5 2.4 collective-permute-done.1
  12.3 1.8 collective-permute-done.3.far_ref
  14.2 3.4 %copy-done.2 = bf16[1024,4096]{1,0:T(8,128)(2,1)S(1)} copy-done((bf16[1024,4096]{1,0:T(8,128)(2,1)S(1)}, bf16[1024,4096]{1,0:T(8,128)(2,1)}, u32[]{:S(2)}) %copy-start.2) | copy-done | bytes 8388632
  18.5 5.4 %attend.1 = (bf16[32,4096]{1,0:T(8,128)(2,1)S(1)}, bf16[32,4096]{1,0:T(8,128)(2,1)S(1)}, bf16[32,4096]{1,0:T(8,128)(2,1)S(1)}, bf16[32,4096]{1,0:T(8,128)(2,1)S(1)}) custom-call(s32[2]{0:T(128)S(1)} %pad_add_fusion.where_ref, bf16[128,1024]{1,0:T(8,128)(2,1)S(1)} %copy-done.3, bf16[512,512]{1,0:T(8,128)(2,1)S(1)} %pad_maximum_fusion.near_ref, ...), custom_call_target="tpu_custom_call" | custom-call | flops 8000000000 | bytes 12582912 | tf_op jit(solution)/shard_map/attend/pallas_call | solution.py:84
  26.2 2.6 collective-permute-start.5
  29.0 9.0 %collective-permute-done.4.rest_1_ = bf16[32,4096]{1,0:T(8,128)(2,1)S(1)} collective-permute-done((bf16[32,4096]{1,0:T(8,128)(2,1)S(1)}, bf16[32,4096]{1,0:T(8,128)(2,1)S(1)}, u32[]{:S(2)}, u32[]{:S(2)}) %collective-permute-start.4) | collective-permute-done | bytes 262176 | tf_op jit(solution)/shard_map/ppermute | solution.py:20
  38.0 9.5 %collective-permute-done.5.rest_2_ = bf16[32,4096]{1,0:T(8,128)(2,1)S(1)} collective-permute-done((bf16[32,4096]{1,0:T(8,128)(2,1)S(1)}, bf16[32,4096]{1,0:T(8,128)(2,1)S(1)}, u32[]{:S(2)}, u32[]{:S(2)}) %collective-permute-start.5) | collective-permute-done | bytes 262176 | tf_op jit(solution)/shard_map/ppermute | solution.py:20
  48.3 2.4 add_and_norm.1
  50.7 6.0 %collective-permute-start.31 = (bf16[32,4096]{1,0:T(8,128)(2,1)}, bf16[32,4096]{1,0:T(8,128)(2,1)S(1)}, u32[]{:S(2)}, u32[]{:S(2)}) collective-permute-start(bf16[32,4096]{1,0:T(8,128)(2,1)} %get-tuple-element.22.refs_0_), channel_id=1, source_target_pairs={{0,2},{1,3},{2,0},{3,1},{4,6},{5,7},{6,4},{7,5},{8,10},{9,11},{10,... | collective-permute-start | bytes 786440 | tf_op jit(solution)/shard_map/ppermute | solution.py:20
  60.3 14.6 %collective-permute-done.31 = bf16[32,4096]{1,0:T(8,128)(2,1)S(1)} collective-permute-done((bf16[32,4096]{1,0:T(8,128)(2,1)}, bf16[32,4096]{1,0:T(8,128)(2,1)S(1)}, u32[]{:S(2)}, u32[]{:S(2)}) %collective-permute-start.31) | collective-permute-done | bytes 262176 | tf_op jit(solution)/shard_map/ppermute | solution.py:20
  78.6 5.6 %collective-permute-done.9.refs_3_ = bf16[32,4096]{1,0:T(8,128)(2,1)S(1)} collective-permute-done((bf16[32,4096]{1,0:T(8,128)(2,1)}, bf16[32,4096]{1,0:T(8,128)(2,1)S(1)}, u32[]{:S(2)}, u32[]{:S(2)}) %collective-permute-start.9) | collective-permute-done | bytes 262176 | tf_op jit(solution)/shard_map/ppermute | solution.py:20
  84.2 2.5 collective-permute-start.33
  86.8 3.9 %collective-permute-done.19.refs_1_ = bf16[32,4096]{1,0:T(8,128)(2,1)S(1)} collective-permute-done((bf16[32,4096]{1,0:T(8,128)(2,1)S(1)}, bf16[32,4096]{1,0:T(8,128)(2,1)S(1)}, u32[]{:S(2)}, u32[]{:S(2)}) %collective-permute-start.19) | collective-permute-done | bytes 262176 | tf_op jit(solution)/shard_map/ppermute | solution.py:20
  90.7 1.7 collective-permute-start.35
  95.5 6.4 %collective-permute-done.33.refs_1_ = bf16[64,4096]{1,0:T(8,128)(2,1)S(1)} collective-permute-done((bf16[64,4096]{1,0:T(8,128)(2,1)S(1)}, bf16[64,4096]{1,0:T(8,128)(2,1)S(1)}, u32[]{:S(2)}, u32[]{:S(2)}) %collective-permute-start.33) | collective-permute-done | bytes 524320 | tf_op jit(solution)/shard_map/ppermute | solution.py:20
  101.9 14.4 %collective-permute-done.34.refs_2_ = bf16[64,4096]{1,0:T(8,128)(2,1)S(1)} collective-permute-done((bf16[64,4096]{1,0:T(8,128)(2,1)S(1)}, bf16[64,4096]{1,0:T(8,128)(2,1)S(1)}, u32[]{:S(2)}, u32[]{:S(2)}) %collective-permute-start.34) | collective-permute-done | bytes 524320 | tf_op jit(solution)/shard_map/ppermute | solution.py:20
  117.7 24.0 %expert_rows.3 = (bf16[128,4096]{1,0:T(8,128)(2,1)S(1)}, bf16[128,4096]{1,0:T(8,128)(2,1)S(1)}) custom-call(bf16[32,4096]{1,0:T(8,128)(2,1)S(1)} %copy-done, bf16[32,4096]{1,0:T(8,128)(2,1)S(1)} %collective-permute-done.7.refs_1_, bf16[32,4096]{1,0:T(8,128)(2,1)S(1)} %collective-permute-done.8.refs_2_, bf16[32,4096]{1,0:T(8,128)(2,1)S(1)} %collective-permute-done.9.refs_3_, ...), custom_call_target="tpu_custom_call" | custom-call | flops 11274289152 | bytes 44040192 | tf_op jit(solution)/shard_map/expert_rows/pallas_call | solution.py:184
  142.9 30.7 %expert_rows.5 = (bf16[256,4096]{1,0:T(8,128)(2,1)S(1)}, bf16[256,4096]{1,0:T(8,128)(2,1)S(1)}) custom-call(bf16[64,4096]{1,0:T(8,128)(2,1)S(1)} %constant_dynamic-update-slice_fusion.2.refs_0_, bf16[64,4096]{1,0:T(8,128)(2,1)S(1)} %collective-permute-done.33.refs_1_, bf16[64,4096]{1,0:T(8,128)(2,1)S(1)} %collective-permute-done.34.refs_2_, ...), custom_call_target="tpu_custom_call" | custom-call | flops 22548578304 | bytes 44040192 | tf_op jit(solution)/shard_map/expert_rows/pallas_call | solution.py:184
  174.2 24.2 %expert_rows.4 = (bf16[128,4096]{1,0:T(8,128)(2,1)S(1)}, bf16[128,4096]{1,0:T(8,128)(2,1)S(1)}) custom-call(bf16[32,4096]{1,0:T(8,128)(2,1)S(1)} %collective-permute-done.18.refs_0_, bf16[32,4096]{1,0:T(8,128)(2,1)S(1)} %collective-permute-done.19.refs_1_, bf16[32,4096]{1,0:T(8,128)(2,1)S(1)} %collective-permute-done.20.refs_2_, ...), custom_call_target="tpu_custom_call" | custom-call | flops 11274289152 | bytes 44040192 | tf_op jit(solution)/shard_map/expert_rows/pallas_call | solution.py:184
  199.5 1.7 collective-permute-start.17
  206.8 8.3 %collective-permute-done.29 = bf16[32,4096]{1,0:T(8,128)(2,1)S(1)} collective-permute-done((bf16[32,4096]{1,0:T(8,128)(2,1)S(1)}, bf16[32,4096]{1,0:T(8,128)(2,1)S(1)}, u32[]{:S(2)}, u32[]{:S(2)}) %collective-permute-start.29) | collective-permute-done | bytes 262176 | tf_op jit(solution)/shard_map/ppermute | solution.py:20
  215.1 1.7 collective-permute-start.43
  216.9 20.2 %collective-permute-done.28 = bf16[32,4096]{1,0:T(8,128)(2,1)S(1)} collective-permute-done((bf16[32,4096]{1,0:T(8,128)(2,1)S(1)}, bf16[32,4096]{1,0:T(8,128)(2,1)S(1)}, u32[]{:S(2)}, u32[]{:S(2)}) %collective-permute-start.28) | collective-permute-done | bytes 262176 | tf_op jit(solution)/shard_map/ppermute | solution.py:20
  237.5 1.9 collective-permute-start.41
  240.5 10.4 %collective-permute-done.42 = bf16[64,4096]{1,0:T(8,128)(2,1)S(1)} collective-permute-done((bf16[64,4096]{1,0:T(8,128)(2,1)S(1)}, bf16[64,4096]{1,0:T(8,128)(2,1)S(1)}, u32[]{:S(2)}, u32[]{:S(2)}) %collective-permute-start.42) | collective-permute-done | bytes 524320 | tf_op jit(solution)/shard_map/ppermute | solution.py:20
  251.0 1.7 collective-permute-start.30
  257.0 3.1 %collective-permute-done.30 = bf16[32,4096]{1,0:T(8,128)(2,1)} collective-permute-done((bf16[32,4096]{1,0:T(8,128)(2,1)}, bf16[32,4096]{1,0:T(8,128)(2,1)}, u32[]{:S(2)}, u32[]{:S(2)}) %collective-permute-start.30) | collective-permute-done | bytes 262176 | tf_op jit(solution)/shard_map/ppermute | solution.py:20
  260.2 7.1 %collective-permute-done.45 = bf16[32,4096]{1,0:T(8,128)(2,1)} collective-permute-done((bf16[32,4096]{1,0:T(8,128)(2,1)}, bf16[32,4096]{1,0:T(8,128)(2,1)}, u32[]{:S(2)}, u32[]{:S(2)}) %collective-permute-start.45) | collective-permute-done | bytes 262176 | tf_op jit(solution)/shard_map/ppermute | solution.py:20
  267.3 10.8 %collective-permute-done.44 = bf16[32,4096]{1,0:T(8,128)(2,1)} collective-permute-done((bf16[32,4096]{1,0:T(8,128)(2,1)}, bf16[32,4096]{1,0:T(8,128)(2,1)}, u32[]{:S(2)}, u32[]{:S(2)}) %collective-permute-start.44) | collective-permute-done | bytes 262176 | tf_op jit(solution)/shard_map/ppermute | solution.py:20
  278.0 2.3 add_convert_fusion.5
  (99 shorter events, 33.0 us)
Async XLA Ops:
  26.2 21.3 %collective-permute-start.5 = (bf16[32,4096]{1,0:T(8,128)(2,1)S(1)}, bf16[32,4096]{1,0:T(8,128)(2,1)S(1)}, u32[]{:S(2)}, u32[]{:S(2)}) collective-permute-start(bf16[32,4096]{1,0:T(8,128)(2,1)S(1)} %get-tuple-element.19), channel_id=1, source_target_pairs={{0,2},{1,3},{2,0},{3,1},{4,6},{5,7},{6,4},{7,5},{8,10},{9,11},{10,... | collective-permute-start | bytes 786440 | tf_op jit(solution)/shard_map/ppermute | solution.py:20
  28.8 18.7 %collective-permute-start.6 = (bf16[32,4096]{1,0:T(8,128)(2,1)S(1)}, bf16[32,4096]{1,0:T(8,128)(2,1)S(1)}, u32[]{:S(2)}, u32[]{:S(2)}) collective-permute-start(bf16[32,4096]{1,0:T(8,128)(2,1)S(1)} %get-tuple-element.20), channel_id=1, source_target_pairs={{0,3},{1,2},{2,1},{3,0},{4,7},{5,6},{6,5},{7,4},{8,11},{9,10},{10,... | collective-permute-start | bytes 786440 | tf_op jit(solution)/shard_map/ppermute | solution.py:20
  50.7 24.2 %collective-permute-start.31 = (bf16[32,4096]{1,0:T(8,128)(2,1)}, bf16[32,4096]{1,0:T(8,128)(2,1)S(1)}, u32[]{:S(2)}, u32[]{:S(2)}) collective-permute-start(bf16[32,4096]{1,0:T(8,128)(2,1)} %get-tuple-element.22.refs_0_), channel_id=1, source_target_pairs={{0,2},{1,3},{2,0},{3,1},{4,6},{5,7},{6,4},{7,5},{8,10},{9,11},{10,... | collective-permute-start | bytes 786440 | tf_op jit(solution)/shard_map/ppermute | solution.py:20
  56.7 19.9 %collective-permute-start.32 = (bf16[32,4096]{1,0:T(8,128)(2,1)}, bf16[32,4096]{1,0:T(8,128)(2,1)S(1)}, u32[]{:S(2)}, u32[]{:S(2)}) collective-permute-start(bf16[32,4096]{1,0:T(8,128)(2,1)} %get-tuple-element.22.refs_0_), channel_id=1, source_target_pairs={{0,3},{1,2},{2,1},{3,0},{4,7},{5,6},{6,5},{7,4},{8,11},{9,10},{10,... | collective-permute-start | bytes 786440 | tf_op jit(solution)/shard_map/ppermute | solution.py:20
  58.1 18.7 %collective-permute-start.18 = (bf16[32,4096]{1,0:T(8,128)(2,1)}, bf16[32,4096]{1,0:T(8,128)(2,1)S(1)}, u32[]{:S(2)}, u32[]{:S(2)}) collective-permute-start(bf16[32,4096]{1,0:T(8,128)(2,1)} %get-tuple-element.22.refs_0_), channel_id=1, source_target_pairs={{0,1},{1,0},{2,3},{3,2},{4,5},{5,4},{6,7},{7,6},{8,9},{9,8},{10,11... | collective-permute-start | bytes 786440 | tf_op jit(solution)/shard_map/ppermute | solution.py:20
  58.1 20.0 %collective-permute-start.7 = (bf16[32,4096]{1,0:T(8,128)(2,1)}, bf16[32,4096]{1,0:T(8,128)(2,1)S(1)}, u32[]{:S(2)}, u32[]{:S(2)}) collective-permute-start(bf16[32,4096]{1,0:T(8,128)(2,1)} %get-tuple-element.22.refs_0_), channel_id=1, source_target_pairs={{0,8},{4,12},{8,0},{12,4},{16,24},{20,28},{24,16},{28,20},{1,9},{5... | collective-permute-start | bytes 786440 | tf_op jit(solution)/shard_map/ppermute | solution.py:20
  59.6 19.0 %collective-permute-start.8 = (bf16[32,4096]{1,0:T(8,128)(2,1)}, bf16[32,4096]{1,0:T(8,128)(2,1)S(1)}, u32[]{:S(2)}, u32[]{:S(2)}) collective-permute-start(bf16[32,4096]{1,0:T(8,128)(2,1)} %get-tuple-element.22.refs_0_), channel_id=1, source_target_pairs={{0,16},{4,20},{8,24},{12,28},{16,0},{20,4},{24,8},{28,12},{1,17},{... | collective-permute-start | bytes 786440 | tf_op jit(solution)/shard_map/ppermute | solution.py:20
  76.7 13.9 %collective-permute-start.19 = (bf16[32,4096]{1,0:T(8,128)(2,1)S(1)}, bf16[32,4096]{1,0:T(8,128)(2,1)S(1)}, u32[]{:S(2)}, u32[]{:S(2)}) collective-permute-start(bf16[32,4096]{1,0:T(8,128)(2,1)S(1)} %collective-permute-done.18.refs_0_), channel_id=1, source_target_pairs={{0,8},{4,12},{8,0},{12,4},{16,24},{20,28},{24,16},{28,20},{1,9},{5... | collective-permute-start | bytes 786440 | tf_op jit(solution)/shard_map/ppermute | solution.py:20
  78.1 14.3 %collective-permute-start.20 = (bf16[32,4096]{1,0:T(8,128)(2,1)S(1)}, bf16[32,4096]{1,0:T(8,128)(2,1)S(1)}, u32[]{:S(2)}, u32[]{:S(2)}) collective-permute-start(bf16[32,4096]{1,0:T(8,128)(2,1)S(1)} %collective-permute-done.18.refs_0_), channel_id=1, source_target_pairs={{0,16},{4,20},{8,24},{12,28},{16,0},{20,4},{24,8},{28,12},{1,17},{... | collective-permute-start | bytes 786440 | tf_op jit(solution)/shard_map/ppermute | solution.py:20
  84.2 17.6 %collective-permute-start.33 = (bf16[64,4096]{1,0:T(8,128)(2,1)S(1)}, bf16[64,4096]{1,0:T(8,128)(2,1)S(1)}, u32[]{:S(2)}, u32[]{:S(2)}) collective-permute-start(bf16[64,4096]{1,0:T(8,128)(2,1)S(1)} %constant_dynamic-update-slice_fusion.2.refs_0_), channel_id=1, source_target_pairs={{0,8},{4,12},{8,0},{12,4},{16,24},{20,28},{24,16},{28,20},{1,9},{5... | collective-permute-start | bytes 1572872 | tf_op jit(solution)/shard_map/ppermute | solution.py:20
  86.8 29.5 %collective-permute-start.34 = (bf16[64,4096]{1,0:T(8,128)(2,1)S(1)}, bf16[64,4096]{1,0:T(8,128)(2,1)S(1)}, u32[]{:S(2)}, u32[]{:S(2)}) collective-permute-start(bf16[64,4096]{1,0:T(8,128)(2,1)S(1)} %constant_dynamic-update-slice_fusion.2.refs_0_), channel_id=1, source_target_pairs={{0,16},{4,20},{8,24},{12,28},{16,0},{20,4},{24,8},{28,12},{1,17},{... | collective-permute-start | bytes 1572872 | tf_op jit(solution)/shard_map/ppermute | solution.py:20
  90.7 25.6 %collective-permute-start.35 = (bf16[64,4096]{1,0:T(8,128)(2,1)S(1)}, bf16[64,4096]{1,0:T(8,128)(2,1)S(1)}, u32[]{:S(2)}, u32[]{:S(2)}) collective-permute-start(bf16[64,4096]{1,0:T(8,128)(2,1)S(1)} %constant_dynamic-update-slice_fusion.2.refs_0_), channel_id=1, source_target_pairs={{0,24},{4,28},{8,16},{12,20},{16,8},{20,12},{24,0},{28,4},{1,25},{... | collective-permute-start | bytes 1572872 | tf_op jit(solution)/shard_map/ppermute | solution.py:20
  93.9 47.9 %collective-permute-start.36 = (bf16[64,4096]{1,0:T(8,128)(2,1)S(1)}, bf16[64,4096]{1,0:T(8,128)(2,1)S(1)}, u32[]{:S(2)}, u32[]{:S(2)}) collective-permute-start(bf16[64,4096]{1,0:T(8,128)(2,1)S(1)} %constant_dynamic-update-slice_fusion.2.refs_0_), channel_id=1, source_target_pairs={{0,4},{4,0},{8,12},{12,8},{16,20},{20,16},{24,28},{28,24},{1,5},{5... | collective-permute-start | bytes 1572872 | tf_op jit(solution)/shard_map/ppermute | solution.py:20
  94.3 47.5 %collective-permute-start.21 = (bf16[32,4096]{1,0:T(8,128)(2,1)S(1)}, bf16[32,4096]{1,0:T(8,128)(2,1)S(1)}, u32[]{:S(2)}, u32[]{:S(2)}) collective-permute-start(bf16[32,4096]{1,0:T(8,128)(2,1)S(1)} %collective-permute-done.18.refs_0_), channel_id=1, source_target_pairs={{0,24},{4,28},{8,16},{12,20},{16,8},{20,12},{24,0},{28,4},{1,25},{... | collective-permute-start | bytes 786440 | tf_op jit(solution)/shard_map/ppermute | solution.py:20
  101.9 40.5 %collective-permute-start.37 = (bf16[64,4096]{1,0:T(8,128)(2,1)S(1)}, bf16[64,4096]{1,0:T(8,128)(2,1)S(1)}, u32[]{:S(2)}, u32[]{:S(2)}) collective-permute-start(bf16[64,4096]{1,0:T(8,128)(2,1)S(1)} %collective-permute-done.33.refs_1_), channel_id=1, source_target_pairs={{0,4},{4,0},{8,12},{12,8},{16,20},{20,16},{24,28},{28,24},{1,5},{5... | collective-permute-start | bytes 1572872 | tf_op jit(solution)/shard_map/ppermute | solution.py:20
  116.2 26.2 %collective-permute-start.38 = (bf16[64,4096]{1,0:T(8,128)(2,1)S(1)}, bf16[64,4096]{1,0:T(8,128)(2,1)S(1)}, u32[]{:S(2)}, u32[]{:S(2)}) collective-permute-start(bf16[64,4096]{1,0:T(8,128)(2,1)S(1)} %collective-permute-done.34.refs_2_), channel_id=1, source_target_pairs={{0,4},{4,0},{8,12},{12,8},{16,20},{20,16},{24,28},{28,24},{1,5},{5... | collective-permute-start | bytes 1572872 | tf_op jit(solution)/shard_map/ppermute | solution.py:20
  116.2 26.6 %collective-permute-start.39 = (bf16[64,4096]{1,0:T(8,128)(2,1)S(1)}, bf16[64,4096]{1,0:T(8,128)(2,1)S(1)}, u32[]{:S(2)}, u32[]{:S(2)}) collective-permute-start(bf16[64,4096]{1,0:T(8,128)(2,1)S(1)} %collective-permute-done.35.refs_3_), channel_id=1, source_target_pairs={{0,4},{4,0},{8,12},{12,8},{16,20},{20,16},{24,28},{28,24},{1,5},{5... | collective-permute-start | bytes 1572872 | tf_op jit(solution)/shard_map/ppermute | solution.py:20
  141.8 31.9 %collective-permute-start.22 = (bf16[32,4096]{1,0:T(8,128)(2,1)S(1)}, bf16[32,4096]{1,0:T(8,128)(2,1)S(1)}, u32[]{:S(2)}, u32[]{:S(2)}) collective-permute-start(bf16[32,4096]{1,0:T(8,128)(2,1)S(1)} %collective-permute-done.18.refs_0_), channel_id=1, source_target_pairs={{0,4},{4,0},{8,12},{12,8},{16,20},{20,16},{24,28},{28,24},{1,5},{5... | collective-permute-start | bytes 786440 | tf_op jit(solution)/shard_map/ppermute | solution.py:20
  141.8 56.7 %collective-permute-start.14 = (bf16[128,4096]{1,0:T(8,128)(2,1)S(1)}, bf16[128,4096]{1,0:T(8,128)(2,1)S(1)}, u32[]{:S(2)}, u32[]{:S(2)}) collective-permute-start(bf16[128,4096]{1,0:T(8,128)(2,1)S(1)} %get-tuple-element.24), channel_id=1, source_target_pairs={{0,4},{4,0},{8,12},{12,8},{16,20},{20,16},{24,28},{28,24},{1,5},{5... | collective-permute-start | bytes 3145736 | tf_op jit(solution)/shard_map/ppermute | solution.py:20
  142.3 31.8 %collective-permute-start.23 = (bf16[32,4096]{1,0:T(8,128)(2,1)S(1)}, bf16[32,4096]{1,0:T(8,128)(2,1)S(1)}, u32[]{:S(2)}, u32[]{:S(2)}) collective-permute-start(bf16[32,4096]{1,0:T(8,128)(2,1)S(1)} %collective-permute-done.19.refs_1_), channel_id=1, source_target_pairs={{0,4},{4,0},{8,12},{12,8},{16,20},{20,16},{24,28},{28,24},{1,5},{5... | collective-permute-start | bytes 786440 | tf_op jit(solution)/shard_map/ppermute | solution.py:20
  142.4 31.7 %collective-permute-start.24 = (bf16[32,4096]{1,0:T(8,128)(2,1)S(1)}, bf16[32,4096]{1,0:T(8,128)(2,1)S(1)}, u32[]{:S(2)}, u32[]{:S(2)}) collective-permute-start(bf16[32,4096]{1,0:T(8,128)(2,1)S(1)} %collective-permute-done.20.refs_2_), channel_id=1, source_target_pairs={{0,4},{4,0},{8,12},{12,8},{16,20},{20,16},{24,28},{28,24},{1,5},{5... | collective-permute-start | bytes 786440 | tf_op jit(solution)/shard_map/ppermute | solution.py:20
  142.9 31.3 %collective-permute-start.25 = (bf16[32,4096]{1,0:T(8,128)(2,1)S(1)}, bf16[32,4096]{1,0:T(8,128)(2,1)S(1)}, u32[]{:S(2)}, u32[]{:S(2)}) collective-permute-start(bf16[32,4096]{1,0:T(8,128)(2,1)S(1)} %collective-permute-done.21.refs_3_), channel_id=1, source_target_pairs={{0,4},{4,0},{8,12},{12,8},{16,20},{20,16},{24,28},{28,24},{1,5},{5... | collective-permute-start | bytes 786440 | tf_op jit(solution)/shard_map/ppermute | solution.py:20
  173.7 31.0 %collective-permute-start.40 = (bf16[256,4096]{1,0:T(8,128)(2,1)S(1)}, bf16[256,4096]{1,0:T(8,128)(2,1)S(1)}, u32[]{:S(2)}, u32[]{:S(2)}) collective-permute-start(bf16[256,4096]{1,0:T(8,128)(2,1)S(1)} %get-tuple-element.28), channel_id=1, source_target_pairs={{0,4},{4,0},{8,12},{12,8},{16,20},{20,16},{24,28},{28,24},{1,5},{5... | collective-permute-start | bytes 6291464 | tf_op jit(solution)/shard_map/ppermute | solution.py:20
  199.5 55.9 %collective-permute-start.17 = (bf16[32,4096]{1,0:T(8,128)(2,1)S(1)}, bf16[32,4096]{1,0:T(8,128)(2,1)S(1)}, u32[]{:S(2)}, u32[]{:S(2)}) collective-permute-start(bf16[32,4096]{1,0:T(8,128)(2,1)S(1)} %get-tuple-element.37), channel_id=1, source_target_pairs={{0,24},{4,28},{8,16},{12,20},{16,8},{20,12},{24,0},{28,4},{1,25},{... | collective-permute-start | bytes 786440 | tf_op jit(solution)/shard_map/ppermute | solution.py:20
  201.2 55.8 %collective-permute-start.16 = (bf16[32,4096]{1,0:T(8,128)(2,1)}, bf16[32,4096]{1,0:T(8,128)(2,1)S(1)}, u32[]{:S(2)}, u32[]{:S(2)}) collective-permute-start(bf16[32,4096]{1,0:T(8,128)(2,1)} %get-tuple-element.38), channel_id=1, source_target_pairs={{0,16},{4,20},{8,24},{12,28},{16,0},{20,4},{24,8},{28,12},{1,17},{... | collective-permute-start | bytes 786440 | tf_op jit(solution)/shard_map/ppermute | solution.py:20
  203.2 33.9 %collective-permute-start.28 = (bf16[32,4096]{1,0:T(8,128)(2,1)S(1)}, bf16[32,4096]{1,0:T(8,128)(2,1)S(1)}, u32[]{:S(2)}, u32[]{:S(2)}) collective-permute-start(bf16[32,4096]{1,0:T(8,128)(2,1)S(1)} %get-tuple-element.41), channel_id=1, source_target_pairs={{0,16},{4,20},{8,24},{12,28},{16,0},{20,4},{24,8},{28,12},{1,17},{... | collective-permute-start | bytes 786440 | tf_op jit(solution)/shard_map/ppermute | solution.py:20
  204.7 32.9 %collective-permute-start.27 = (bf16[32,4096]{1,0:T(8,128)(2,1)S(1)}, bf16[32,4096]{1,0:T(8,128)(2,1)S(1)}, u32[]{:S(2)}, u32[]{:S(2)}) collective-permute-start(bf16[32,4096]{1,0:T(8,128)(2,1)S(1)} %get-tuple-element.39), channel_id=1, source_target_pairs={{0,8},{4,12},{8,0},{12,4},{16,24},{20,28},{24,16},{28,20},{1,9},{5... | collective-permute-start | bytes 786440 | tf_op jit(solution)/shard_map/ppermute | solution.py:20
  215.1 25.2 %collective-permute-start.43 = (bf16[64,4096]{1,0:T(8,128)(2,1)S(1)}, bf16[64,4096]{1,0:T(8,128)(2,1)S(1)}, u32[]{:S(2)}, u32[]{:S(2)}) collective-permute-start(bf16[64,4096]{1,0:T(8,128)(2,1)S(1)} %get-tuple-element.34), channel_id=1, source_target_pairs={{0,24},{4,28},{8,16},{12,20},{16,8},{20,12},{24,0},{28,4},{1,25},{... | collective-permute-start | bytes 1572872 | tf_op jit(solution)/shard_map/ppermute | solution.py:20
  237.1 13.9 %collective-permute-start.42 = (bf16[64,4096]{1,0:T(8,128)(2,1)S(1)}, bf16[64,4096]{1,0:T(8,128)(2,1)S(1)}, u32[]{:S(2)}, u32[]{:S(2)}) collective-permute-start(bf16[64,4096]{1,0:T(8,128)(2,1)S(1)} %get-tuple-element.35), channel_id=1, source_target_pairs={{0,16},{4,20},{8,24},{12,28},{16,0},{20,4},{24,8},{28,12},{1,17},{... | collective-permute-start | bytes 1572872 | tf_op jit(solution)/shard_map/ppermute | solution.py:20
  237.5 15.1 %collective-permute-start.41 = (bf16[64,4096]{1,0:T(8,128)(2,1)S(1)}, bf16[64,4096]{1,0:T(8,128)(2,1)S(1)}, u32[]{:S(2)}, u32[]{:S(2)}) collective-permute-start(bf16[64,4096]{1,0:T(8,128)(2,1)S(1)} %get-tuple-element.33), channel_id=1, source_target_pairs={{0,8},{4,12},{8,0},{12,4},{16,24},{20,28},{24,16},{28,20},{1,9},{5... | collective-permute-start | bytes 1572872 | tf_op jit(solution)/shard_map/ppermute | solution.py:20
  240.3 16.7 %collective-permute-start.15 = (bf16[32,4096]{1,0:T(8,128)(2,1)S(1)}, bf16[32,4096]{1,0:T(8,128)(2,1)}, u32[]{:S(2)}, u32[]{:S(2)}) collective-permute-start(bf16[32,4096]{1,0:T(8,128)(2,1)S(1)} %get-tuple-element.36), channel_id=1, source_target_pairs={{0,8},{4,12},{8,0},{12,4},{16,24},{20,28},{24,16},{28,20},{1,9},{5... | collective-permute-start | bytes 786440 | tf_op jit(solution)/shard_map/ppermute | solution.py:20
  255.4 22.7 %collective-permute-start.44 = (bf16[32,4096]{1,0:T(8,128)(2,1)}, bf16[32,4096]{1,0:T(8,128)(2,1)}, u32[]{:S(2)}, u32[]{:S(2)}) collective-permute-start(bf16[32,4096]{1,0:T(8,128)(2,1)} %get-tuple-element.42), channel_id=1, source_target_pairs={{0,2},{1,3},{2,0},{3,1},{4,6},{5,7},{6,4},{7,5},{8,10},{9,11},{10,... | collective-permute-start | bytes 786440 | tf_op jit(solution)/shard_map/ppermute | solution.py:20
  (24 other events, 199.4 us)
